TPU v7x, 1024 devices: a whole 8x8x8 slice. The times are simulated.
1024 devices in a mesh: occ: 64 (over z, x), aux: 16 (over y, core).
Axes of the slice: x: 8, y: 8, z: 8, core: 2. Of those that a mesh axis runs over, the one named last changes fastest.
Arguments:
- ri_blocks: bfloat16 [64, 48, 16384], P('occ', None, 'aux'), may hold values from -0.29882812 to 0.29882812
- blk_occ: int32 [64], replicated, may hold values from 0 to 39
- blk_virt: int32 [64], replicated, may hold values from 0 to 255
- live_count: int32 [64], replicated, may hold values from 1 to 48
- aux_mask: int32 [64, 64], replicated, may hold values 0 or 1
- occ_energy: float32 [40], replicated, may hold values from -2 to -0.3
- virt_energy: float32 [12288], replicated, may hold values from 0.1 to 3
- frequency: float32 [1], replicated, may hold values from 0.2 to 2
Outputs:
- response: float32 [16384, 16384], P('occ', 'aux')
All inputs are finite; a program needn't handle non-finite values.
Results may differ from a plain program's by a relative error of at most 0.0028.
Values may be sent and summed in bfloat16 or wider, within the bound.
A program may use at most 64 MiB of HBM per device.

v0:
```python
import jax
import jax.numpy as jnp
from jax import lax
from jax.sharding import PartitionSpec as P


def pair_weights(occ_ids, virt_ids, counts, occ_energy, virt_energy, frequency, depth):
    virt_table = virt_energy.reshape(-1, depth)
    energy_gap = virt_table[virt_ids] - occ_energy[occ_ids][:, None]
    is_live = lax.broadcasted_iota(jnp.int32, energy_gap.shape, 1) < counts[:, None]
    return jnp.where(
        is_live,
        2.0 * energy_gap / (energy_gap * energy_gap + frequency[0] * frequency[0]),
        jnp.zeros_like(energy_gap),
    )


def per_device(
    ri_blocks, blk_occ, blk_virt, live_count, aux_mask, occ_energy, virt_energy, frequency
):
    n_blocks, n_rows, n_cols = ri_blocks.shape
    groups = aux_mask.shape[1]
    aux_block = n_cols * lax.axis_size("aux") // groups
    here_groups = n_cols // aux_block
    group_first = lax.axis_index("aux") * here_groups
    block_first = lax.axis_index("occ") * n_blocks
    local_live = lax.dynamic_slice_in_dim(aux_mask, group_first, here_groups, 1)
    local_live = lax.dynamic_slice_in_dim(local_live, block_first, n_blocks, 0)
    shaped = ri_blocks.reshape(n_blocks, n_rows, here_groups, aux_block)
    kept_blocks = jnp.where(
        local_live[:, None, :, None] == 1, shaped, jnp.zeros_like(shaped)
    ).reshape(n_blocks, n_rows, n_cols)
    row_parts = lax.all_to_all(kept_blocks, "occ", split_axis=2, concat_axis=0, tiled=True)
    row_side = lax.all_gather(row_parts, "aux", axis=2, tiled=True)
    local_weights = pair_weights(
        lax.dynamic_slice_in_dim(blk_occ, block_first, n_blocks, 0),
        lax.dynamic_slice_in_dim(blk_virt, block_first, n_blocks, 0),
        lax.dynamic_slice_in_dim(live_count, block_first, n_blocks, 0),
        occ_energy,
        virt_energy,
        frequency,
        n_rows,
    )
    scaled_here = (local_weights[:, :, None] * kept_blocks).astype(jnp.bfloat16)
    return jnp.einsum(
        "bri,brj->ij",
        row_side,
        lax.all_gather(scaled_here, "occ", axis=0, tiled=True),
        preferred_element_type=jnp.float32,
    )


def solution(mesh):
    placed = (P("occ", None, "aux"), P(), P(), P(), P(), P(), P(), P())
    return jax.shard_map(
        per_device, mesh=mesh, in_specs=placed, out_specs=P("occ", "aux"), check_vma=False
    )
```

profile of v0, /device:TPU:1, one launch (start us, length us, event | category | flops | bytes accessed | tf_op | source)
XLA Modules:
  0.0 218.6 jit_solution(14327038148185460252)
XLA Ops:
  6.5 0.0 all-gather.6.cloned.1.call-start
  6.5 1.2 dynamic_slice.16
  8.9 1.2 dynamic_slice.15
  11.4 1.2 dynamic_slice.14
  12.7 0.9 reshape.79
  14.2 0.8 compare_bitcast_fusion
  15.0 0.1 broadcast_in_dim.28
  15.7 1.3 dynamic-slice.6
  17.6 1.3 compare_select_fusion
  18.9 1.6 multiply_convert_fusion
  20.5 0.4 copy.25
  20.9 0.5 broadcast.94
  21.4 2.3 %reduce = bf16[1024,48]{1,0:T(8,128)(2,1)S(1)} reduce(bf16[1024,1,48]{2,1,0:T(2,128)(2,1)S(1)} %bitcast.22, bf16[]{:T(256)} %broadcast.94), dimensions={1}, to_apply=%bitcast.19.reduce_sub_computation | reduce | bytes 196610
  23.7 0.4 reshape.123
  24.1 34.4 %all_to_all.18 = bf16[64,2,384]{2,1,0:T(2,128)(2,1)S(1)} all-to-all(bf16[64,2,384]{2,1,0:T(2,128)(2,1)S(1)} %reshape.123), channel_id=1, replica_groups=mesh['occ'=64,'aux'=16] {'occ'}, dimensions={0} | all-to-all | bytes 196608 | tf_op jit(solution)/shard_map/all_to_all | solution.py:33
  58.4 0.5 reshape.124
  59.0 0.9 copy.26
  59.9 0.0 all-gather.6.cloned.1.call-update
  60.0 0.2 all-gather.4.cloned.1.call-start
  60.2 0.5 all-gather.4.cloned.1.call-update
  60.7 39.5 %all-gather.6.cloned.1.call-done = bf16[64,1,48,256]{0,2,1,3:T(8,128)(2,1)} async-done(((bf16[64,1,48,16]{0,2,1,3:T(8,128)(2,1)}), bf16[64,1,48,256]{0,2,1,3:T(8,128)(2,1)}) %all-gather.6.cloned.1.call-update) | async-done | bytes 1572880 | tf_op jit(solution)/shard_map/all_gather | solution.py:34
  100.2 4.1 %copy.27 = bf16[64,1,48,256]{3,0,2,1:T(8,128)(2,1)S(1)} copy(bf16[64,1,48,256]{0,2,1,3:T(8,128)(2,1)} %all-gather.6.cloned.1.call-done) | data formatting | bytes 3145728 | tf_op jit(solution)/shard_map/all_gather | solution.py:34
  104.3 96.5 %all-gather.4.cloned.1.call-done = bf16[64,48,1024]{2,1,0:T(8,128)(2,1)} async-done(((bf16[1,48,1024]{2,1,0:T(8,128)(2,1)}), bf16[64,48,1024]{2,1,0:T(8,128)(2,1)}) %all-gather.4.cloned.1.call-update) | async-done | bytes 6291472 | tf_op jit(solution)/shard_map/all_gather | solution.py:48
  200.8 11.0 %fusion.3 = f32[256,1024]{1,0:T(8,128)} fusion(bf16[64,48,1024]{2,1,0:T(8,128)(2,1)} %all-gather.4.cloned.1.call-done, bf16[64,1,48,256]{3,0,2,1:T(8,128)(2,1)S(1)} %copy.27), kind=kOutput, calls=%fused_computation.3 | convolution fusion | flops 1610612736 | bytes 8912896 | tf_op jit(solution)/shard_map/bri,brj->ij/dot_general | solution.py:45
  (2 shorter events, 0.1 us)
Async XLA Ops:
  6.5 93.7 %all-gather.6.cloned.1.call-start = ((), (), s32[]{:S(2)}) async-start(), calls=%async_computation.2 | async-start | bytes 3342336 | tf_op jit(solution)/shard_map/all_gather | solution.py:34
  60.0 140.8 %all-gather.4.cloned.1.call-start = ((), (), s32[]{:S(2)}) async-start(), calls=%async_computation.1 | async-start | bytes 6389760 | tf_op jit(solution)/shard_map/all_gather | solution.py:48
Sparse Core Ops, SparseCore 0:
  60.1 40.0 all-gather.5
  104.4 96.3 all-gather.3
where the time goes:
time: 219 us
  waiting for transfers between devices  136 us (62%)
  blocking collectives  34.4 us (16%)
  between operations  17.8 us (8%)
  local copies, waits for them, and re-layouts  12.8 us (6%)
  matrix products  11 us (5%)
  other arithmetic  5.92 us (3%)
    all_gather x1, waiting for transfers between devices, per_device(): lax.all_gather(scaled_here, 'occ', axis=0, tiled=True)  96.5 us
    all_gather x1, waiting for transfers between devices, per_device(): row_side = lax.all_gather(row_parts, 'aux', axis=2, tiled=True)  39.5 us
    all_to_all x1, blocking collectives, per_device(): lax.all_to_all(kept_blocks, 'occ', split_axis=2, concat_axis=0, tiled=True)  34.4 us
    dot_general x1, matrix products, per_device(): jnp.einsum('bri,brj->ij', row_side, lax.all_gather(scaled_here, 'occ', ax...  11 us
  transfers between devices with their start and end apart: 2, of which 2 were waited for; matrix products, arithmetic and copies ran while one was open for 2% of the time, Pallas kernels for 0%

commit v1 on v0

v1 whole, which is shorter than its diff:
```python
import functools

import jax
import jax.numpy as jnp
from jax import lax
from jax.experimental import pallas as pl
from jax.experimental.pallas import tpu as pltpu
from jax.sharding import PartitionSpec as P

MESH = pl.DeviceIdType.MESH
F32 = jnp.float32
BF16 = jnp.bfloat16


def offset_of(slot):
    return (1 - 2 * (slot % 2)) * ((slot + 1) // 2)


def kernel(
    n, ny, aux_block,
    occ_ids, virt_ids, counts, mask, occ_energy, frequency, virt_ref, x_ref,
    out_ref,
    ga, gb, scaled, rows, wide, virt_rows, meta_shift, meta_count, meta_occ, weight_t,
    recv_a, recv_b, send_sem, y_recv, y_send, p_recv, p_send,
):
    _, depth, cols = x_ref.shape
    half = cols // 2
    run = rows.shape[2]
    far = n // 2
    bundle = n * depth
    o = lax.axis_index("occ")
    a = lax.axis_index("aux")
    z, x = o // n, o % n
    y, core = a // 2, a % 2
    late = z // far

    xp, xm = z * n + (x + 1) % n, z * n + (x + n - 1) % n
    zp, zm = ((z + 1) % n) * n + x, ((z + n - 1) % n) * n + x
    partner = y * 2 + (1 - core)

    barrier = pltpu.get_barrier_semaphore()
    for dest in (xp, xm, zp, zm):
        pl.semaphore_signal(barrier, inc=1, device_id=(dest, a), device_id_type=MESH)
    for d in range(1, ny):
        pl.semaphore_signal(
            barrier, inc=1, device_id=(o, ((y + d) % ny) * 2 + core), device_id_type=MESH
        )
    pl.semaphore_signal(barrier, inc=1, device_id=(o, partner), device_id_type=MESH)

    per_half = half // aux_block
    for k in range(2 * per_half):
        live = mask[o, a * 2 * per_half + k] == 1
        part = x_ref[0, :, k * aux_block:(k + 1) * aux_block]
        part = jnp.where(live, part, jnp.zeros_like(part))
        target, at = (ga, k) if k < per_half else (gb, k - per_half)
        target[0, 0, :, at * aux_block:(at + 1) * aux_block] = part

    pl.semaphore_wait(barrier, 4 + ny - 1 + 1)

    def left(d):
        return 2 * d - 1

    def right(d):
        return 2 * d if d < far else n - 1

    def hop(buf, recv, kind, src, dst, dest):
        pltpu.make_async_remote_copy(
            src_ref=buf.at[src],
            dst_ref=buf.at[dst],
            send_sem=send_sem.at[kind],
            recv_sem=recv.at[dst],
            device_id=(dest, a),
            device_id_type=MESH,
        ).start()

    def arrived(buf, recv, slot):
        pltpu.make_async_copy(buf.at[slot], buf.at[slot], recv.at[slot]).wait()

    plans = (
        (ga, recv_a, 0, zp, zm, far, far - 1, xp, xm),
        (gb, recv_b, 4, xp, xm, far - 1, far, zp, zm),
    )

    def spread(plan, i):
        buf, recv, kind, _, _, _, _, onward, backward = plan
        hop(buf, recv, kind + 2, (0, i), (left(1), i), onward)
        hop(buf, recv, kind + 3, (0, i), (right(1), i), backward)

    for plan in plans:
        buf, recv, kind, up, down = plan[:5]
        hop(buf, recv, kind, (0, 0), (0, left(1)), up)
        hop(buf, recv, kind + 1, (0, 0), (0, right(1)), down)
    for plan in plans:
        spread(plan, 0)

    def fetch(p, carry):
        oj, oi = offset_of(p // n), offset_of(p % n)
        bz = (z + oi + late * (oj - oi) + n) % n
        bx = (x + oj + late * (oi - oj) + n) % n
        b = bz * n + bx
        first = virt_ids[b] * depth
        line = first // 128
        virt_rows[0, pl.ds(p, 1), :] = virt_ref[pl.ds(line, 1), :]
        virt_rows[1, pl.ds(p, 1), :] = virt_ref[
            pl.ds(jnp.minimum(line + 1, virt_ref.shape[0] - 1), 1), :
        ]
        meta_shift[pl.ds(p, 1), :] = jnp.full((1, 128), first - line * 128, jnp.int32)
        meta_count[pl.ds(p, 1), :] = jnp.full((1, 128), counts[b], jnp.int32)
        meta_occ[pl.ds(p, 1), :] = jnp.full((1, 128), occ_energy[occ_ids[b]], F32)
        return carry

    lax.fori_loop(0, n * n, fetch, 0)
    shift = meta_shift[...]
    energy = jnp.zeros(shift.shape, F32)
    pairs = jnp.concatenate([virt_rows[0], virt_rows[1]], axis=1)
    for k in range(8):
        energy = jnp.where(shift == 16 * k, pairs[:, 16 * k:16 * k + 128], energy)
    gap = energy - meta_occ[...]
    freq = frequency[0]
    lane = lax.broadcasted_iota(jnp.int32, shift.shape, 1)
    weight = jnp.where(
        lane < meta_count[...], 2.0 * gap / (gap * gap + freq * freq), jnp.zeros_like(gap)
    )
    weight = jnp.concatenate([weight, jnp.zeros((128 - n * n, 128), F32)], axis=0)
    weight_t[...] = weight.T
    for p in range(n * n):
        wide[p * depth:(p + 1) * depth, :] = jnp.broadcast_to(
            weight_t[0:depth, p:p + 1], (depth, 128)
        )

    for d in range(1, far + 1):
        for plan in plans:
            buf, recv, kind, up, down, up_limit, down_limit = plan[:7]
            if d <= up_limit:
                arrived(buf, recv, (0, left(d)))
                if d < up_limit:
                    hop(buf, recv, kind, (0, left(d)), (0, left(d + 1)), up)
                spread(plan, left(d))
            if d <= down_limit:
                arrived(buf, recv, (0, right(d)))
                if d < down_limit:
                    hop(buf, recv, kind + 1, (0, right(d)), (0, right(d + 1)), down)
                spread(plan, right(d))

    def scale(which, j, i):
        buf = (ga, gb)[which]
        in_order = j * n + i
        swapped = i * n + j
        swap = late if which == 0 else 1 - late
        row = pl.multiple_of((in_order + swap * (swapped - in_order)) * depth, 16)
        w = wide[pl.ds(row, depth), :]
        for t in range(half // 128):
            piece = buf[j, i, :, t * 128:(t + 1) * 128].astype(F32)
            start = which * half + t * 128
            scaled[pl.ds(row, depth), start:start + 128] = (w * piece).astype(BF16)

    tile = pl.multiple_of((o % (n * n // 2)) * run // 128 * 128, 128)
    pick = (
        lax.broadcasted_iota(jnp.int32, (run, 128), 1)
        == lax.broadcasted_iota(jnp.int32, (run, 128), 0) + (o * run) % 128
    ).astype(BF16)

    def slots_of(s):
        return (0, 1) if s == 0 else ((2 * s - 1, 2 * s + 1) if s < far else (n - 1, n))

    def lanes_of(s):
        first, last = slots_of(s)
        return slice(first * bundle, last * bundle)

    def cut(s):
        first, last = slots_of(s)
        for j in range(first, last):
            from_a = ga[j, :, :, pl.ds(tile, 128)].reshape(bundle, 128)
            from_b = gb[j, :, :, pl.ds(tile, 128)].reshape(bundle, 128)
            block = jnp.where(late == 1, from_b, from_a)
            slab = lax.dot_general(
                pick, block, (((1,), (1,)), ((), ())), preferred_element_type=F32
            )
            rows[y, core, :, j * bundle:(j + 1) * bundle] = slab.astype(BF16)
        mine = rows.at[y, core, :, lanes_of(s)]
        for d in range(1, ny):
            pltpu.make_async_remote_copy(
                src_ref=mine,
                dst_ref=mine,
                send_sem=y_send.at[s],
                recv_sem=y_recv.at[s],
                device_id=(o, ((y + d) % ny) * 2 + core),
                device_id_type=MESH,
            ).start()

    def others(s):
        return rows.at[0:ny - 1, 0, :, lanes_of(s)]

    def pass_on(s):
        pltpu.make_async_copy(others(s), others(s), y_recv.at[s]).wait()
        ours = rows.at[:, core, :, lanes_of(s)]
        pltpu.make_async_remote_copy(
            src_ref=ours,
            dst_ref=ours,
            send_sem=p_send.at[s],
            recv_sem=p_recv.at[s],
            device_id=(o, partner),
            device_id_type=MESH,
        ).start()

    def rows_here(s):
        theirs = rows.at[:, 1 - core, :, lanes_of(s)]
        pltpu.make_async_copy(theirs, theirs, p_recv.at[s]).wait()

    n_rows = out_ref.shape[0]
    tile_n = min(256, half)

    def multiply(which, s, fresh):
        k = lanes_of(s)

        def body(t, carry):
            at = pl.ds(pl.multiple_of(which * half + t * tile_n, 128), tile_n)
            part = jnp.dot(
                rows[:, :, :, k].reshape(n_rows, k.stop - k.start),
                scaled[k, at],
                preferred_element_type=F32,
            )
            if fresh:
                out_ref[:, at] = part
            else:
                out_ref[:, at] += part
            return carry

        lax.fori_loop(0, half // tile_n, body, 0)

    def own_units(i, carry):
        scale(0, 0, i)
        scale(1, 0, i)
        return carry

    lax.fori_loop(0, n, own_units, 0)
    cut(0)
    for s in range(1, far + 1):
        def pair(i2, carry):
            for parity in range(2):
                i = 2 * i2 + parity
                for which, plan in enumerate(plans):
                    buf, recv, kind = plan[:3]
                    onward, backward = plan[7:]
                    up_limit, down_limit = far - parity, far - 1 + parity
                    if s <= up_limit:
                        arrived(buf, recv, (left(s), i))
                        if s < up_limit:
                            hop(buf, recv, kind + 2, (left(s), i), (left(s + 1), i), onward)
                    if s <= down_limit:
                        arrived(buf, recv, (right(s), i))
                        if s < down_limit:
                            hop(buf, recv, kind + 3, (right(s), i), (right(s + 1), i), backward)
                for which in range(2):
                    if s <= up_limit:
                        scale(which, left(s), i)
                    if s <= down_limit:
                        scale(which, right(s), i)
            return carry

        lax.fori_loop(0, n // 2, pair, 0)
        cut(s)
        pass_on(s - 1)
        if s >= 2:
            rows_here(s - 2)
            multiply(late, s - 2, s == 2)
    rows_here(far - 1)
    multiply(late, far - 1, False)
    for s in range(far):
        multiply(1 - late, s, s == 0)
    pass_on(far)
    rows_here(far)
    multiply(late, far, False)
    multiply(1 - late, far, False)

    for plan in plans:
        buf, _, kind, _, _, up_limit, down_limit, _, _ = plan
        flat = ((kind, up_limit), (kind + 1, down_limit))
        for sem, count in flat:
            sent = buf.at[0, 0:count]
            pltpu.make_async_copy(sent, sent, send_sem.at[sem]).wait()
        for sem in (kind + 2, kind + 3):
            sent = buf.at[0:n - 1, 0:n // 2]
            pltpu.make_async_copy(sent, sent, send_sem.at[sem]).wait()
    for s in range(far + 1):
        pltpu.make_async_copy(others(s), others(s), y_send.at[s]).wait()
        ours = rows.at[:, core, :, lanes_of(s)]
        pltpu.make_async_copy(ours, ours, p_send.at[s]).wait()


def solution(mesh):
    n = 1
    while n * n < mesh.shape["occ"]:
        n += 1
    ny = mesh.shape["aux"] // 2
    far = n // 2

    def per_device(ri, occ_ids, virt_ids, counts, mask, occ_energy, virt_energy, frequency):
        _, depth, cols = ri.shape
        run = cols // (n * n)
        n_rows = 2 * ny * run
        total = n * n * depth
        aux_block = cols * 2 * ny // mask.shape[1]
        smem = pl.BlockSpec(memory_space=pltpu.SMEM)
        vmem = pl.BlockSpec(memory_space=pltpu.VMEM)
        return pl.pallas_call(
            functools.partial(kernel, n, ny, aux_block),
            out_shape=jax.ShapeDtypeStruct((n_rows, cols), F32),
            in_specs=[smem] * 6 + [vmem] * 2,
            out_specs=vmem,
            scratch_shapes=[
                pltpu.VMEM((n, n, depth, cols // 2), BF16),
                pltpu.VMEM((n, n, depth, cols // 2), BF16),
                pltpu.VMEM((total, cols), BF16),
                pltpu.VMEM((ny, 2, run, total), BF16),
                pltpu.VMEM((total, 128), F32),
                pltpu.VMEM((2, n * n, 128), F32),
                pltpu.VMEM((n * n, 128), jnp.int32),
                pltpu.VMEM((n * n, 128), jnp.int32),
                pltpu.VMEM((n * n, 128), F32),
                pltpu.VMEM((128, 128), F32),
                pltpu.SemaphoreType.DMA((n, n)),
                pltpu.SemaphoreType.DMA((n, n)),
                pltpu.SemaphoreType.DMA((8,)),
                pltpu.SemaphoreType.DMA((far + 1,)),
                pltpu.SemaphoreType.DMA((far + 1,)),
                pltpu.SemaphoreType.DMA((far + 1,)),
                pltpu.SemaphoreType.DMA((far + 1,)),
            ],
            compiler_params=pltpu.CompilerParams(
                collective_id=0, has_side_effects=True, vmem_limit_bytes=48 * 1024 * 1024
            ),
            name="response",
        )(
            occ_ids, virt_ids, counts, mask, occ_energy, frequency,
            virt_energy.reshape(-1, 128), ri,
        )

    placed = (P("occ", None, "aux"), P(), P(), P(), P(), P(), P(), P())
    return jax.shard_map(
        per_device, mesh=mesh, in_specs=placed, out_specs=P("occ", "aux"), check_vma=False
    )
```

time: 219 us -> 78.8 us (0.36)
  waiting for transfers between devices: 136 us -> 0 us
  Pallas kernels: 0 us -> 73.7 us
  blocking collectives: 34.4 us -> 0 us
  between operations: 17.8 us -> 0.71 us
  matrix products: 11 us -> 0 us
  local copies, waits for them, and re-layouts: 12.8 us -> 4.08 us
  other arithmetic: 5.92 us -> 0 us
    all_gather x2 -> x0, waiting for transfers between devices: 136 us -> none  [the longest x1 96.5 us: per_device(): lax.all_gather(scaled_here, 'occ', axis=0, tiled=True)]
    pallas_call x0 -> x1, Pallas kernels: none -> 73.7 us  [per_device(): pl.pallas_call(functools.partial(kernel, n, ny, aux_block), out_shape=jax...]
    all_to_all x1 -> x0, blocking collectives: 34.4 us -> none  [per_device(): lax.all_to_all(kept_blocks, 'occ', split_axis=2, concat_axis=0, tiled=True)]
    dot_general x1 -> x0, matrix products: 11 us -> none  [per_device(): jnp.einsum('bri,brj->ij', row_side, lax.all_gather(scaled_here, 'occ', ax...]
    all_gather x1 -> x0, local copies, waits for them, and re-layouts: 4.07 us -> none  [per_device(): row_side = lax.all_gather(row_parts, 'aux', axis=2, tiled=True)]
    dynamic_slice x3 -> x0, local copies, waits for them, and re-layouts: 3.71 us -> none  [the longest x1 1.24 us: per_device(): lax.dynamic_slice_in_dim(blk_virt, block_first, n_blocks, 0)]
    unnamed x4 -> x15, local copies, waits for them, and re-layouts: 1.45 us -> 4.08 us
    unnamed x1 -> x0, other arithmetic: 2.27 us -> none
  transfers between devices with their start and end apart: 2 -> 0, of which waited for: 2 -> 0; matrix products, arithmetic and copies ran while one was open for 2% -> 0% of each run, Pallas kernels for 0% -> 0%
where the time goes in v1:
time: 78.8 us; the launch traced here: 78.5 us
  Pallas kernels  73.7 us (94%)
  local copies, waits for them, and re-layouts  4.08 us (5%)
    pallas_call x1, Pallas kernels, per_device(): pl.pallas_call(functools.partial(kernel, n, ny, aux_block), out_shape=jax...  73.7 us
    unnamed x15, local copies, waits for them, and re-layouts  4.08 us

profile of v1, /device:TPU:1, one launch (start us, length us, event | category | flops | bytes accessed | tf_op | source)
XLA Modules:
  0.0 78.5 jit_solution(6247462152525758983)
XLA Ops:
  0.0 0.0 copy-start.6
  0.7 0.0 copy-start.3
  0.7 0.0 copy-start.4
  0.7 0.0 copy-start.5
  0.7 0.0 copy-done.6
  0.7 0.6 copy-done.3
  1.3 0.0 copy-done.4
  1.3 0.0 copy-done.5
  1.4 0.0 copy-start
  1.4 0.9 %copy-done = bf16[1,48,1024]{2,1,0:T(8,128)(2,1)S(1)} copy-done((bf16[1,48,1024]{2,1,0:T(8,128)(2,1)S(1)}, bf16[1,48,1024]{2,1,0:T(8,128)(2,1)}, u32[]{:S(2)}) %copy-start) | copy-done | bytes 98328
  2.2 0.0 copy-start.1
  2.3 0.8 %copy-done.1 = f32[12288]{0:T(1024)S(1)} copy-done((f32[12288]{0:T(1024)S(1)}, f32[12288]{0:T(1024)}, u32[]{:S(2)}) %copy-start.1) | copy-done | bytes 49176
  3.0 0.0 copy-start.2
  3.1 0.8 copy-done.2
  3.8 73.7 %response.1 = f32[256,1024]{1,0:T(8,128)S(1)} custom-call(s32[64]{0:T(128)S(1)} %copy-done.3, s32[64]{0:T(128)S(1)} %copy-done.4, s32[64]{0:T(128)S(1)} %copy-done.5, s32[64,64]{1,0:T(8,128)S(1)} %copy-done.2, f32[40]{0:T(128)S(1)} %copy-done.6, f32[1]{0:T(128)S(6)} %copy.10.frequency, f32[96,128]{1,0:T(8,128)S(1)} %bitcast.1, bf16[1,48,1024]{2,1,0:T(8,128)(2,1)S(1)} %copy-done), custom_call_target="tpu_custom_call" | custom-call | tf_op jit(solution)/shard_map/response/pallas_call | solution.py:306
  77.5 1.0 %copy.11 = f32[256,1024]{1,0:T(8,128)} copy(f32[256,1024]{1,0:T(8,128)S(1)} %response.1) | data formatting | bytes 2097152
Async XLA Ops:
  0.0 0.7 copy-start.6
  0.7 0.7 copy-start.3
  0.7 0.7 copy-start.4
  0.7 0.7 copy-start.5
  1.4 0.9 %copy-start = (bf16[1,48,1024]{2,1,0:T(8,128)(2,1)S(1)}, bf16[1,48,1024]{2,1,0:T(8,128)(2,1)}, u32[]{:S(2)}) copy-start(bf16[1,48,1024]{2,1,0:T(8,128)(2,1)} %x_ref.1) | copy-start | bytes 294916
  2.2 0.8 %copy-start.1 = (f32[12288]{0:T(1024)S(1)}, f32[12288]{0:T(1024)}, u32[]{:S(2)}) copy-start(f32[12288]{0:T(1024)} %param.14) | copy-start | bytes 147460
  3.0 0.8 copy-start.2

commit v2 on v0

v2 whole, which is shorter than its diff:
```python
import functools

import jax
import jax.numpy as jnp
from jax import lax
from jax.experimental import pallas as pl
from jax.experimental.pallas import tpu as pltpu
from jax.sharding import PartitionSpec as P

MESH = pl.DeviceIdType.MESH
F32 = jnp.float32
BF16 = jnp.bfloat16
POINTS = (0, 6, 10)
MOST = 13


def offset_of(slot):
    return (1 - 2 * (slot % 2)) * ((slot + 1) // 2)


def kernel(
    n, ny, aux_block,
    occ_ids_in, virt_ids_in, counts_in, mask_in, occ_energy_in, frequency_in, virt_in, x_in,
    out_ref,
    ga, gb, scaled, last, rows, tail, mine, tiles, runs, wide,
    occ_ids, virt_ids, counts, occ_energy, frequency, mask, virt,
    virt_rows, meta_shift, meta_count, meta_occ, weight_t,
    recv_a, recv_b, send_sem, load_sem, t_recv, t_send, r_recv, r_send,
    y_recv, y_send, p_recv, p_send,
):
    depth, half = ga.shape[2:]
    run = rows.shape[3]
    far = n // 2
    bundle = n * depth
    o = lax.axis_index("occ")
    a = lax.axis_index("aux")
    z, x = o // n, o % n
    y, core = a // 2, a % 2

    def at_x(d):
        return z * n + (x + d + n) % n

    def at_z(d):
        return ((z + d + n) % n) * n + x

    def at_y(d):
        return (y + d + ny) % ny

    xp, xm, zp, zm = at_x(1), at_x(-1), at_z(1), at_z(-1)
    partner = y * 2 + (1 - core)
    near = sorted({d % ny for d in (1, -1, 2, -2)} - {0})

    loads = [
        pltpu.make_async_copy(src, dst, load_sem.at[k])
        for k, (src, dst) in enumerate((
            (mask_in, mask),
            (x_in.at[0, :, 0:half], ga.at[0, 0]),
            (x_in.at[0, :, half:2 * half], gb.at[0, 0]),
            (occ_ids_in, occ_ids),
            (virt_ids_in, virt_ids),
            (counts_in, counts),
            (occ_energy_in, occ_energy),
            (frequency_in, frequency),
            (virt_in, virt),
        ))
    ]
    for load in loads:
        load.start()

    barrier = pltpu.get_barrier_semaphore()
    for d in range(1, n):
        for dest in (at_x(d), at_z(d)):
            pl.semaphore_signal(barrier, inc=1, device_id=(dest, a), device_id_type=MESH)
    for d in near:
        pl.semaphore_signal(
            barrier, inc=1, device_id=(o, at_y(d) * 2 + core), device_id_type=MESH
        )
    pl.semaphore_signal(barrier, inc=1, device_id=(o, partner), device_id_type=MESH)

    for load in loads[:3]:
        load.wait()
    mask_row = mask[pl.ds(o, 1), :]
    mask_lane = lax.broadcasted_iota(jnp.int32, mask_row.shape, 1)
    per_half = half // aux_block
    for k in range(2 * per_half):
        live = jnp.sum(
            jnp.where(mask_lane == a * 2 * per_half + k, mask_row, 0), axis=1, keepdims=True
        )
        target, at = (ga, k) if k < per_half else (gb, k - per_half)
        place = slice(at * aux_block, (at + 1) * aux_block)
        part = target[0, 0, :, place]
        keep = jnp.broadcast_to(live, part.shape) == 1
        part = jnp.where(keep, part, jnp.zeros_like(part))
        target[0, 0, :, place] = part
        for t in range(max(1, aux_block // 128)):
            if aux_block >= 128:
                mine[k * aux_block // 128 + t] = part[:, t * 128:(t + 1) * 128]
            else:
                low = k * aux_block % 128
                mine[k * aux_block // 128, :, low:low + aux_block] = part

    pl.semaphore_wait(barrier, 2 * (n - 1) + len(near) + 1)

    def left(d):
        return 2 * d - 1

    def right(d):
        return 2 * d if d < far else n - 1

    def remote(src, dst, send, recv, dest):
        pltpu.make_async_remote_copy(
            src_ref=src, dst_ref=dst, send_sem=send, recv_sem=recv,
            device_id=dest, device_id_type=MESH,
        ).start()

    def settle(ref, sem):
        pltpu.make_async_copy(ref, ref, sem).wait()

    def hop(buf, recv, kind, src, dst, dest):
        remote(buf.at[src], buf.at[dst], send_sem.at[kind], recv.at[dst], (dest, a))

    def arrived(buf, recv, slot):
        settle(buf.at[slot], recv.at[slot])

    plans = (
        (ga, recv_a, 0, zp, zm, far, far - 1, xp, xm),
        (gb, recv_b, 4, xp, xm, far - 1, far, zp, zm),
    )

    def spread(plan, i):
        buf, recv, kind, _, _, _, _, onward, backward = plan
        hop(buf, recv, kind + 2, (0, i), (left(1), i), onward)
        hop(buf, recv, kind + 3, (0, i), (right(1), i), backward)

    for plan in plans:
        buf, recv, kind, up, down = plan[:5]
        hop(buf, recv, kind, (0, 0), (0, left(1)), up)
        hop(buf, recv, kind + 1, (0, 0), (0, right(1)), down)
    own_tile = z * n * run // 128
    for j in range(1, n):
        k = (z - offset_of(j) + n) % n
        remote(mine.at[k * n * run // 128], tiles.at[j], t_send, t_recv, (k * n + x, a))
    tiles[0] = mine[own_tile]
    for plan in plans:
        spread(plan, 0)

    def fetch(p, carry):
        oj, oi = offset_of(p // n), offset_of(p % n)
        b = ((z + oi + n) % n) * n + (x + oj + n) % n
        first = virt_ids[b] * depth
        line = first // 128
        virt_rows[0, pl.ds(p, 1), :] = virt[pl.ds(line, 1), :]
        virt_rows[1, pl.ds(p, 1), :] = virt[pl.ds(jnp.minimum(line + 1, virt.shape[0] - 1), 1), :]
        meta_shift[pl.ds(p, 1), :] = jnp.full((1, 128), first - line * 128, jnp.int32)
        meta_count[pl.ds(p, 1), :] = jnp.full((1, 128), counts[b], jnp.int32)
        meta_occ[pl.ds(p, 1), :] = jnp.full((1, 128), occ_energy[occ_ids[b]], F32)
        return carry

    def cut():
        settle(tiles.at[1:n], t_recv)
        lane = lax.broadcasted_iota(jnp.int32, (128, 128), 1)
        line = lax.broadcasted_iota(jnp.int32, (128, 128), 0)
        pick = (lane == line + z * n * run % 128).astype(BF16)
        block = tiles[...].reshape(bundle, 128)
        turned = lax.dot_general(
            pick, block, (((1,), (1,)), ((), ())), preferred_element_type=F32
        ).astype(BF16)
        runs[...] = turned[0:n * run].reshape(runs.shape)
        for j in range(1, n):
            k = (x - offset_of(j) + n) % n
            remote(runs.at[k], rows.at[y, core, j], r_send, r_recv, (z * n + k, a))
        rows[y, core, 0] = runs[x]

    for load in loads[3:]:
        load.wait()
    for d in range(1, far + 1):
        landed = []
        for plan in plans:
            buf, recv, kind, up, down, up_limit, down_limit = plan[:7]
            if d <= up_limit:
                arrived(buf, recv, (0, left(d)))
                if d < up_limit:
                    hop(buf, recv, kind, (0, left(d)), (0, left(d + 1)), up)
                landed.append((plan, left(d)))
            if d <= down_limit:
                arrived(buf, recv, (0, right(d)))
                if d < down_limit:
                    hop(buf, recv, kind + 1, (0, right(d)), (0, right(d + 1)), down)
                landed.append((plan, right(d)))
        for plan, i in landed:
            spread(plan, i)
        if d == 1:
            cut()
        if d < far:
            share = -(-n * n // (far - 1))
            lax.fori_loop(share * (d - 1), min(share * d, n * n), fetch, 0)

    shift = meta_shift[...]
    energy = jnp.zeros(shift.shape, F32)
    both = jnp.concatenate([virt_rows[0], virt_rows[1]], axis=1)
    for k in range(8):
        energy = jnp.where(shift == 16 * k, both[:, 16 * k:16 * k + 128], energy)
    gap = energy - meta_occ[...]
    freq = frequency[0]
    weight = jnp.where(
        lax.broadcasted_iota(jnp.int32, shift.shape, 1) < meta_count[...],
        2.0 * gap / (gap * gap + freq * freq),
        jnp.zeros_like(gap),
    )
    weight = jnp.concatenate([weight, jnp.zeros((128 - n * n, 128), F32)], axis=0)
    weight_t[...] = weight.T
    for p in range(n * n):
        wide[p * depth:(p + 1) * depth, :] = jnp.broadcast_to(
            weight_t[0:depth, p:p + 1], (depth, 128)
        )

    def order(which, j, i):
        return j * n + i if which == 0 else i * n + j

    def scale(which, j, i, apart=False):
        buf = (ga, gb)[which]
        row = pl.multiple_of(order(which, j, i) * depth, 16)
        w = wide[pl.ds(row, depth), :]
        for t in range(half // 128):
            place = slice(t * 128, (t + 1) * 128)
            piece = (w * buf[j, i, :, place].astype(F32)).astype(BF16)
            if apart:
                last[which, pl.ds(pl.multiple_of(i * depth, 16), depth), place] = piece
            else:
                scaled[which, pl.ds(row, depth), place] = piece

    def own_slab(d):
        return rows.at[at_y(d), core]

    def pass_slab(d, by):
        remote(
            own_slab(d), own_slab(d), y_send, y_recv.at[(d - by) % ny],
            (o, at_y(by) * 2 + core),
        )

    def to_partner(d):
        remote(own_slab(d), own_slab(d), p_send, p_recv, (o, partner))

    relay = ((-1, 2), (1, -2), (-2, 2)) if ny > 5 else ()

    def ring_point(stage):
        if stage == 0:
            settle(rows.at[0, 0, 0:n - 1], r_recv)
            for d in near:
                pass_slab(0, d)
            to_partner(0)
        elif stage == 1:
            for d in near:
                settle(own_slab(d), y_recv.at[d])
            for d, by in relay:
                pass_slab(d, by)
            for d in near:
                to_partner(d)
        else:
            for d, by in relay:
                settle(own_slab(d - by), y_recv.at[(d - by) % ny])
                to_partner(d - by)

    n_rows = out_ref.shape[0]
    tile_n = min(256, half)

    def each_tile(body):
        lax.fori_loop(0, half // tile_n, lambda t, c: (body(t), c)[1], 0)

    def multiply_most(which):
        def body(t):
            part = pl.ds(pl.multiple_of(t * tile_n, 128), tile_n)

            to = pl.ds(pl.multiple_of(which * half + t * tile_n, 128), tile_n)
            for j in range(0, n, 2):
                pair_of = [rows[:, :, j + k].reshape(n_rows, bundle) for k in range(2)]
                part_sum = jnp.dot(
                    jnp.concatenate(pair_of, axis=1),
                    scaled[which, j * bundle:(j + 2) * bundle, part],
                    preferred_element_type=F32,
                )
                if j == 0:
                    out_ref[:, to] = part_sum
                else:
                    out_ref[:, to] += part_sum

        each_tile(body)

    def multiply_last(which):
        def body(t):
            part = pl.ds(pl.multiple_of(t * tile_n, 128), tile_n)
            to = pl.ds(pl.multiple_of(which * half + t * tile_n, 128), tile_n)
            out_ref[:, to] += jnp.dot(
                tail[which], last[which, :, part], preferred_element_type=F32
            )

        each_tile(body)

    def own_units(i, carry):
        scale(0, 0, i)
        scale(1, 0, i)
        return carry

    lax.fori_loop(0, n, own_units, 0)
    for which in range(2):
        for i in range(n):
            row = pl.multiple_of(order(which, n - 1, i) * depth, 16)
            scaled[which, pl.ds(row, depth), :] = jnp.zeros((depth, half), BF16)

    def second(s, first, stop):
        def pair(i2, carry):
            for parity in range(2):
                i = 2 * i2 + parity
                up_limit, down_limit = far - parity, far - 1 + parity
                for plan in plans:
                    buf, recv, kind = plan[:3]
                    onward, backward = plan[7:]
                    if s <= up_limit:
                        arrived(buf, recv, (left(s), i))
                        if s < up_limit:
                            hop(buf, recv, kind + 2, (left(s), i), (left(s + 1), i), onward)
                    if s <= down_limit:
                        arrived(buf, recv, (right(s), i))
                        if s < down_limit:
                            hop(buf, recv, kind + 3, (right(s), i), (right(s + 1), i), backward)
            for parity in range(2):
                i = 2 * i2 + parity
                up_limit, down_limit = far - parity, far - 1 + parity
                for which in range(2):
                    if s <= up_limit:
                        scale(which, left(s), i, s == far)
                    if s <= down_limit:
                        scale(which, right(s), i, s == far)
            return carry

        lax.fori_loop(first, stop, pair, 0)

    pairs_of = n // 2
    points, most = (POINTS, MOST) if n == 8 else ((0, 1, 2), 3)
    stops = {points[1]: 1, points[2]: 2}
    ring_point(0)
    for s in range(1, far + 1):
        first = 0
        for stop in range(1, pairs_of + 1):
            count = (s - 1) * pairs_of + stop
            if stop == pairs_of or count in stops or count == most:
                second(s, first, stop)
                first = stop
            if count in stops:
                ring_point(stops[count])
            if count == most:
                settle(rows.at[:, 1 - core], p_recv)
                tail[0] = rows[:, :, n - 1].reshape(n_rows, bundle)
                tail[1] = jnp.concatenate(
                    [
                        rows[:, :, i].reshape(n_rows, bundle)[:, (n - 1) * depth:]
                        for i in range(n)
                    ],
                    axis=1,
                )
                multiply_most(0)
                multiply_most(1)
    multiply_last(0)
    multiply_last(1)

    for plan in plans:
        buf, _, kind, _, _, up_limit, down_limit, _, _ = plan
        settle(buf.at[0, 0:up_limit], send_sem.at[kind])
        settle(buf.at[0, 0:down_limit], send_sem.at[kind + 1])
        for sem in (kind + 2, kind + 3):
            settle(buf.at[0:n - 1, 0:n // 2], send_sem.at[sem])

    settle(tiles.at[1:n], t_send)
    settle(runs.at[1:n], r_send)
    settle(rows.at[0:ny - 1, 0], y_send)
    settle(rows.at[:, core], p_send)


def solution(mesh):
    n = 1
    while n * n < mesh.shape["occ"]:
        n += 1
    ny = mesh.shape["aux"] // 2

    def per_device(ri, occ_ids, virt_ids, counts, mask, occ_energy, virt_energy, frequency):
        _, depth, cols = ri.shape
        run = cols // (n * n)
        n_rows = 2 * ny * run
        total = n * n * depth
        half = cols // 2
        aux_block = cols * 2 * ny // mask.shape[1]
        virt = virt_energy.reshape(-1, 128)
        dma = pltpu.SemaphoreType.DMA
        return pl.pallas_call(
            functools.partial(kernel, n, ny, aux_block),
            out_shape=jax.ShapeDtypeStruct((n_rows, cols), F32),
            in_specs=[pl.BlockSpec(memory_space=pltpu.HBM)] * 8,
            out_specs=pl.BlockSpec(memory_space=pltpu.VMEM),
            scratch_shapes=[
                pltpu.VMEM((n, n, depth, half), BF16),
                pltpu.VMEM((n, n, depth, half), BF16),
                pltpu.VMEM((2, total, half), BF16),
                pltpu.VMEM((2, n * depth, half), BF16),
                pltpu.VMEM((ny, 2, n, run, n * depth), BF16),
                pltpu.VMEM((2, n_rows, n * depth), BF16),
                pltpu.VMEM((cols // 128, depth, 128), BF16),
                pltpu.VMEM((n, depth, 128), BF16),
                pltpu.VMEM((n, run, n * depth), BF16),
                pltpu.VMEM((total, 128), F32),
                pltpu.SMEM(occ_ids.shape, jnp.int32),
                pltpu.SMEM(virt_ids.shape, jnp.int32),
                pltpu.SMEM(counts.shape, jnp.int32),
                pltpu.SMEM(occ_energy.shape, F32),
                pltpu.SMEM(frequency.shape, F32),
                pltpu.VMEM(mask.shape, jnp.int32),
                pltpu.VMEM(virt.shape, F32),
                pltpu.VMEM((2, n * n, 128), F32),
                pltpu.VMEM((n * n, 128), jnp.int32),
                pltpu.VMEM((n * n, 128), jnp.int32),
                pltpu.VMEM((n * n, 128), F32),
                pltpu.VMEM((128, 128), F32),
                dma((n, n)), dma((n, n)), dma((8,)), dma((9,)),
                dma, dma, dma, dma, dma((ny,)), dma, dma, dma,
            ],
            compiler_params=pltpu.CompilerParams(
                collective_id=0, has_side_effects=True, vmem_limit_bytes=60 * 1024 * 1024
            ),
            name="response",
        )(occ_ids, virt_ids, counts, mask, occ_energy, frequency, virt, ri)

    placed = (P("occ", None, "aux"), P(), P(), P(), P(), P(), P(), P())
    return jax.shard_map(
        per_device, mesh=mesh, in_specs=placed, out_specs=P("occ", "aux"), check_vma=False
    )
```

time: 219 us -> 68.7 us (0.31)
  the two profiles are of different devices: /device:TPU:1 before, /device:TPU:4 now
where the time goes in v2:
time: 68.7 us; the launch traced here: 68.5 us
  Pallas kernels  65.5 us (95%)
  local copies, waits for them, and re-layouts  2.31 us (3%)
    pallas_call x1, Pallas kernels, per_device(): pl.pallas_call(functools.partial(kernel, n, ny, aux_block), out_shape=jax...  65.5 us
    unnamed x1, local copies, waits for them, and re-layouts  2.31 us

profile of v2, /device:TPU:4, one launch (start us, length us, event | category | flops | bytes accessed | tf_op | source)
XLA Modules:
  0.0 68.5 jit_solution(12802676784788733434)
XLA Ops:
  0.7 65.5 %response.1 = f32[256,1024]{1,0:T(8,128)} custom-call(s32[64]{0:T(128)} %occ_ids_in.1, s32[64]{0:T(128)} %virt_ids_in.1, s32[64]{0:T(128)} %counts_in.1, s32[64,64]{1,0:T(8,128)} %mask_in.1, f32[40]{0:T(128)} %occ_energy_in.1, f32[1]{0:T(128)S(6)} %copy.10.frequency_in, f32[96,128]{1,0:T(8,128)} %bitcast.1, bf16[1,48,1024]{2,1,0:T(8,128)(2,1)} %x_in.1), custom_call_target="tpu_custom_call" | custom-call | tf_op jit(solution)/shard_map/response/pallas_call | solution.py:394
  66.2 2.3 %copy.11 = f32[256,1024]{1,0:T(8,128)} copy(f32[256,1024]{1,0:T(8,128)} %response.1) | data formatting | bytes 2097152

commit v3 on v2

--- a/solution.py
+++ b/solution.py
@@ -124,7 +124,7 @@
 
     plans = (
         (ga, recv_a, 0, zp, zm, far, far - 1, xp, xm),
-        (gb, recv_b, 4, xp, xm, far - 1, far, zp, zm),
+        (gb, recv_b, 4, xp, xm, far, far - 1, zp, zm),
     )
 
     def spread(plan, i):
@@ -423,10 +423,13 @@
                 dma, dma, dma, dma, dma((ny,)), dma, dma, dma,
             ],
             compiler_params=pltpu.CompilerParams(
-                collective_id=0, has_side_effects=True, vmem_limit_bytes=60 * 1024 * 1024
+                collective_id=0, has_side_effects=True, vmem_limit_bytes=48 * 1024 * 1024
             ),
             name="response",
-        )(occ_ids, virt_ids, counts, mask, occ_energy, frequency, virt, ri)
+        )(*(
+            v if v is frequency else pltpu.with_memory_space_constraint(v, pltpu.HBM)
+            for v in (occ_ids, virt_ids, counts, mask, occ_energy, frequency, virt, ri)
+        ))
 
     placed = (P("occ", None, "aux"), P(), P(), P(), P(), P(), P(), P())
     return jax.shard_map(

time: 68.7 us -> 65.9 us (0.959)
  the two profiles are of different devices: /device:TPU:4 before, /device:TPU:1 now
where the time goes in v3:
time: 65.9 us; the launch traced here: 64.6 us
  Pallas kernels  62.9 us (95%)
  local copies, waits for them, and re-layouts  0.97 us (1%)
  between operations  0.66 us (1%)
    pallas_call x1, Pallas kernels, per_device(): pl.pallas_call(functools.partial(kernel, n, ny, aux_block), out_shape=jax...  62.9 us

profile of v3, /device:TPU:1, one launch (start us, length us, event | category | flops | bytes accessed | tf_op | source)
XLA Modules:
  0.0 64.6 jit_solution(5087292322124038648)
XLA Ops:
  0.7 62.9 %response.1 = f32[256,1024]{1,0:T(8,128)S(1)} custom-call(s32[64]{0:T(128)} %occ_ids_in.1, s32[64]{0:T(128)} %virt_ids_in.1, s32[64]{0:T(128)} %counts_in.1, s32[64,64]{1,0:T(8,128)} %mask_in.1, f32[40]{0:T(128)} %occ_energy_in.1, f32[1]{0:T(128)S(6)} %copy.10.frequency_in, f32[96,128]{1,0:T(8,128)} %bitcast.1, bf16[1,48,1024]{2,1,0:T(8,128)(2,1)} %x_in.1), custom_call_target="tpu_custom_call" | custom-call | tf_op jit(solution)/shard_map/response/pallas_call | solution.py:394
  63.6 1.0 %copy.11 = f32[256,1024]{1,0:T(8,128)} copy(f32[256,1024]{1,0:T(8,128)S(1)} %response.1) | data formatting | bytes 2097152
